TPU v7x, 128 devices: a whole 4x4x4 slice. The times are simulated.
128 devices in a mesh: dp: 8 (over y, core), vocab: 16 (over x, z).
Axes of the slice: x: 4, y: 4, z: 4, core: 2. Of those that a mesh axis runs over, the one named last changes fastest.
Arguments:
- latent_vectors: bfloat16 [1024, 7168], P('dp'), may hold values from -80 to 80
- unembedding_matrix: bfloat16 [7168, 129280], P(None, ('dp', 'vocab')), may hold values from -0.19921875 to 0.19921875
- softmax_divisor: float32 [1024], P('dp'), may hold values from 0.5 to 1.5
- top_probability_quota: int32 [1024], P('dp'), may hold values from 50 to 99
Outputs:
- nucleus: float32 [1024, 129280], P(None, ('dp', 'vocab'))
All inputs are finite; a program needn't handle non-finite values.
Results may differ from a plain program's by a relative error of at most 0.00185.
Values may be sent and summed in bfloat16 or wider, within the bound.
A program may use at most 128 MiB of HBM per device.

v0:
```python
import jax
import jax.numpy as jnp
from jax import lax
from jax.sharding import PartitionSpec as P

BISECT_PASSES = 4
PROBES = 4


soft_width = 0.25
sharpness = 0.02
initial_level = -16.0
first_spacing = 4.0


def merged(value, axis, join):
    pieces = jax.tree.map(lambda part: lax.all_gather(part, axis), value)
    head = jax.tree.map(lambda part: part[0], pieces)
    tail = jax.tree.map(lambda part: part[1:], pieces)
    running, _ = lax.scan(lambda running, piece: (join(running, piece), None), head, tail)
    return running


def combine_stats(first, second):
    peak = jnp.maximum(first[0], second[0])
    summed_mass = first[1] * jnp.exp(first[0] - peak) + second[1] * jnp.exp(second[0] - peak)
    return (peak, summed_mass)


def nucleus_rows(unnormalized_energies, level, stats_fn, masses_fn, kept_fn):
    local_top = jnp.max(unnormalized_energies, axis=1)
    local_sum = jnp.sum(jnp.exp(unnormalized_energies - local_top[:, None]), axis=1)
    top, total = stats_fn((local_top, local_sum))
    shifted = unnormalized_energies - top[:, None]
    prob = jnp.exp(shifted) / total[:, None]
    lower = jnp.full(level.shape, initial_level, jnp.float32)
    level_spacing = first_spacing
    for round_index in range(BISECT_PASSES):
        offsets = level_spacing * jnp.arange(1, PROBES + 1, dtype=jnp.float32)
        cutoffs = lower[:, None] + offsets[None, :]
        shard_probability_share = jnp.stack(
            [
                jnp.sum(
                    prob * jax.nn.sigmoid((shifted - cutoffs[:, probe : probe + 1]) / soft_width),
                    axis=1,
                )
                for probe in range(PROBES)
            ],
            axis=1,
        )
        masses = masses_fn(shard_probability_share)
        passed = jnp.sum(jax.nn.sigmoid((masses - level[:, None]) / sharpness), axis=1)
        estimate = lower + level_spacing * passed
        level_spacing = level_spacing / 2.0
        lower = estimate - level_spacing
    nucleus_cutoff = lower + 2.0 * level_spacing
    weight = prob * jax.nn.sigmoid((shifted - nucleus_cutoff[:, None]) / soft_width)
    kept = kept_fn(jnp.sum(weight, axis=1))
    return weight / kept[:, None]


def on_device(latent_vectors, unembedding_matrix, softmax_divisor, top_probability_quota):
    level = top_probability_quota.astype(jnp.float32) / 100.0
    raw_logits = jnp.dot(
        lax.all_gather(latent_vectors, "dp", axis=0, tiled=True),
        unembedding_matrix,
        preferred_element_type=jnp.float32,
    )
    every_temp, every_level = (
        lax.all_gather(softmax_divisor, "dp", axis=0, tiled=True),
        lax.all_gather(level, "dp", axis=0, tiled=True),
    )
    unnormalized_energies = raw_logits / every_temp[:, None]
    return nucleus_rows(
        unnormalized_energies,
        every_level,
        lambda pair: merged(pair, ("dp", "vocab"), combine_stats),
        lambda shard_probability_share: lax.psum(shard_probability_share, ("dp", "vocab")),
        lambda local_kept: lax.psum(local_kept, ("dp", "vocab")),
    )


def solution(mesh):
    placed = (P("dp", None), P(None, ("dp", "vocab")), P("dp"), P("dp"))
    return jax.shard_map(
        on_device, mesh=mesh, in_specs=placed, out_specs=P(None, ("dp", "vocab")), check_vma=False
    )
```

profile of v0, /device:TPU:1, one launch (start us, length us, event | category | flops | bytes accessed | tf_op | source)
XLA Modules:
  0.0 583.8 jit_solution(10225159048321979590)
XLA Ops:
  6.5 0.0 all-gather.6.cloned.1.call-start
  6.5 0.7 all-gather.6.cloned.1.call-update
  7.3 12.2 %all-gather.2 = f32[8,1,128]{2,1,0:T(1,128)S(1)} all-gather(f32[1,1,128]{2,1,0:T(1,128)} %bitcast.80), channel_id=1, replica_groups=mesh['dp'=8,'vocab'=16] {'dp'}, dimensions={0}, use_global_device_ids=true | all-gather | bytes 4608 | tf_op jit(solution)/shard_map/all_gather | solution.py:70
  19.5 0.7 multiply_bitcast_fusion
  20.1 8.0 %all-gather.3 = f32[8,1,128]{2,1,0:T(1,128)S(1)} all-gather(f32[1,1,128]{2,1,0:T(1,128)S(1)} %multiply_bitcast_fusion), channel_id=1, replica_groups=mesh['dp'=8,'vocab'=16] {'dp'}, dimensions={0}, use_global_device_ids=true | all-gather | bytes 4608 | tf_op jit(solution)/shard_map/all_gather | solution.py:71
  28.2 0.7 fusion.8
  28.9 60.0 %all-gather.6.cloned.1.call-done = bf16[1024,7168]{1,0:T(8,128)(2,1)} async-done(((bf16[128,7168]{1,0:T(8,128)(2,1)}), bf16[1024,7168]{1,0:T(8,128)(2,1)}) %all-gather.6.cloned.1.call-update) | async-done | bytes 14680080 | tf_op jit(solution)/shard_map/all_gather | solution.py:65
  88.9 20.0 %fusion.9 = (f32[1024]{0:T(1024)S(1)}, f32[1024,1010]{0,1:T(8,128)S(1)}) fusion(f32[1024]{0:T(1024)S(1)} %bitcast.51, bf16[1024,7168]{1,0:T(8,128)(2,1)} %all-gather.6.cloned.1.call-done, bf16[7168,1010]{0,1:T(8,128)(2,1)} %param.7), kind=kOutput, calls=%fused_computation.54 | convolution fusion | flops 14828932096 | bytes 33304576 | tf_op jit(solution)/shard_map/dot_general | solution.py:64
  108.9 0.0 copy-start
  108.9 2.0 copy-done
  110.9 0.6 exponential_reduce_fusion
  111.5 52.4 %all-gather.1 = f32[131072]{0:T(1024)S(1)} all-gather(f32[1024]{0:T(1024)S(1)} %exponential_reduce_fusion), channel_id=3, replica_groups=mesh['dp'=8,'vocab'=16] {'dp','vocab'}, dimensions={0}, use_global_device_ids=true | all-gather | bytes 528384 | tf_op jit(solution)/shard_map/all_gather | solution.py:17
  164.0 51.1 %all-gather = f32[131072]{0:T(1024)S(1)} all-gather(f32[1024]{0:T(1024)S(1)} %get-tuple-element.83), channel_id=2, replica_groups=mesh['dp'=8,'vocab'=16] {'dp','vocab'}, dimensions={0}, use_global_device_ids=true | all-gather | bytes 528384 | tf_op jit(solution)/shard_map/all_gather | solution.py:17
  215.2 0.1 reshape.60
  215.3 0.1 reshape.59
  215.4 6.9 %while.12 = (s32[]{:T(128)}, f32[1024]{0:T(1024)S(1)}, f32[1024]{0:T(1024)S(1)}, f32[127,1024]{1,0:T(8,128)S(1)}, f32[127,1024]{1,0:T(8,128)S(1)}, /*index=5*/s32[]{:T(128)}) while((s32[]{:T(128)}, f32[1024]{0:T(1024)S(1)}, f32[1024]{0:T(1024)S(1)}, f32[127,1024]{1,0:T(8,128)S(1)}, f32[127,1024]{1,0:T(8,128)S(1)}, /*index=5*/s32[]{:T(128)}) %tuple.50), condition=%wide.region_3.4_spmd, body=%wide.region_2.3_spmd.sunk | while | flops 6146 | bytes 41033 | solution.py:20
  222.3 8.8 %multiply_reduce_fusion.15 = (f32[1024]{0:T(1024)S(1)}, f32[1024]{0:T(1024)S(1)}, f32[1024]{0:T(1024)S(1)}, f32[1024]{0:T(1024)S(1)}) fusion(f32[]{:T(128)} %bitcast.4, f32[1024,1010]{0,1:T(8,128)} %copy-done, f32[1024]{0:T(1024)S(1)} %get-tuple-element.33, f32[1024]{0:T(1024)S(1)} %get-tuple-element.34, f32[]{:T(128)} %bitcast.6, f32[]{:T(128)} %bitcast.8, ...), kind=kLoop, calls=%fused_computation.19 | loop fusion | flops 31023104 | bytes 4161552 | tf_op jit(solution)/shard_map/reduce_sum | solution.py:43
  231.1 64.3 %psum.35 = f32[1024,4]{0,1:T(4,128)S(1)} all-reduce(f32[1024,4]{0,1:T(4,128)S(1)} %pad_maximum_fusion), channel_id=1, replica_groups=mesh['dp'=8,'vocab'=16] {'dp','vocab'}, use_global_device_ids=true, to_apply=%region_8.9 | all-reduce | flops 4096 | bytes 32768 | tf_op jit(solution)/shard_map/psum | solution.py:78
  295.4 0.1 broadcast_add_fusion.2
  295.5 6.2 %multiply_reduce_fusion.11 = (f32[1024]{0:T(1024)S(1)}, f32[1024]{0:T(1024)S(1)}, f32[1024]{0:T(1024)S(1)}, f32[1024]{0:T(1024)S(1)}) fusion(f32[1024]{0:T(1024)S(1)} %bitcast.55, f32[1024,1010]{0,1:T(8,128)} %copy-done, f32[1024]{0:T(1024)S(1)} %get-tuple-element.33, f32[1024]{0:T(1024)S(1)} %get-tuple-element.34, f32[1024]{0:T(1024)S(1)} %bitcast.54, ...), kind=kLoop, calls=%fused_computation.15 | loop fusion | flops 31023104 | bytes 4177920 | tf_op jit(solution)/shard_map/reduce_sum | solution.py:43
  301.8 63.4 %psum.36 = f32[1024,4]{0,1:T(4,128)S(1)} all-reduce(f32[1024,4]{0,1:T(4,128)S(1)} %pad_maximum_fusion.1), channel_id=1, replica_groups=mesh['dp'=8,'vocab'=16] {'dp','vocab'}, use_global_device_ids=true, to_apply=%region_14.15 | all-reduce | flops 4096 | bytes 32768 | tf_op jit(solution)/shard_map/psum | solution.py:78
  365.2 0.1 broadcast_add_fusion.1
  365.3 6.2 %multiply_reduce_fusion.7 = (f32[1024]{0:T(1024)S(1)}, f32[1024]{0:T(1024)S(1)}, f32[1024]{0:T(1024)S(1)}, f32[1024]{0:T(1024)S(1)}) fusion(f32[1024]{0:T(1024)S(1)} %bitcast.59, f32[1024,1010]{0,1:T(8,128)} %copy-done, f32[1024]{0:T(1024)S(1)} %get-tuple-element.33, f32[1024]{0:T(1024)S(1)} %get-tuple-element.34, f32[1024]{0:T(1024)S(1)} %bitcast.58, ...), kind=kLoop, calls=%fused_computation.11 | loop fusion | flops 31023104 | bytes 4177920 | tf_op jit(solution)/shard_map/reduce_sum | solution.py:43
  371.5 63.1 %psum.37 = f32[1024,4]{0,1:T(4,128)S(1)} all-reduce(f32[1024,4]{0,1:T(4,128)S(1)} %pad_maximum_fusion.2), channel_id=1, replica_groups=mesh['dp'=8,'vocab'=16] {'dp','vocab'}, use_global_device_ids=true, to_apply=%region_20.21 | all-reduce | flops 4096 | bytes 32768 | tf_op jit(solution)/shard_map/psum | solution.py:78
  434.7 0.1 broadcast_add_fusion
  434.8 6.2 %multiply_reduce_fusion.3 = (f32[1024]{0:T(1024)S(1)}, f32[1024]{0:T(1024)S(1)}, f32[1024]{0:T(1024)S(1)}, f32[1024]{0:T(1024)S(1)}) fusion(f32[1024]{0:T(1024)S(1)} %bitcast.63, f32[1024,1010]{0,1:T(8,128)} %copy-done, f32[1024]{0:T(1024)S(1)} %get-tuple-element.33, f32[1024]{0:T(1024)S(1)} %get-tuple-element.34, f32[1024]{0:T(1024)S(1)} %bitcast.62, ...), kind=kLoop, calls=%fused_computation.7 | loop fusion | flops 31023104 | bytes 4177920 | tf_op jit(solution)/shard_map/reduce_sum | solution.py:43
  441.0 63.5 %psum.38 = f32[1024,4]{0,1:T(4,128)S(1)} all-reduce(f32[1024,4]{0,1:T(4,128)S(1)} %pad_maximum_fusion.3), channel_id=1, replica_groups=mesh['dp'=8,'vocab'=16] {'dp','vocab'}, use_global_device_ids=true, to_apply=%region_26.27 | all-reduce | flops 4096 | bytes 32768 | tf_op jit(solution)/shard_map/psum | solution.py:78
  504.6 4.6 fusion.4
  509.2 62.7 %psum.39 = f32[1024]{0:T(1024)S(1)} all-reduce(f32[1024]{0:T(1024)S(1)} %get-tuple-element.63), channel_id=1, replica_groups=mesh['dp'=8,'vocab'=16] {'dp','vocab'}, use_global_device_ids=true, to_apply=%region_29.30 | all-reduce | flops 1024 | bytes 8192 | tf_op jit(solution)/shard_map/psum | solution.py:79
  571.9 5.1 broadcast_divide_fusion
  (277 shorter events, 3.7 us)
Async XLA Ops:
  6.5 82.3 %all-gather.6.cloned.1.call-start = ((), (), s32[]{:S(2)}) async-start(), calls=%async_computation | async-start | bytes 16515072 | tf_op jit(solution)/shard_map/all_gather | solution.py:65
  108.9 2.0 copy-start
Sparse Core Ops, SparseCore 0:
  9.0 79.7 all-gather.5
where the time goes:
time: 585 us; the launch traced here: 584 us
  blocking collectives  441 us (75%)
  waiting for transfers between devices  60.7 us (10%)
  other arithmetic  40.2 us (7%)
  matrix products  20 us (3%)
  between operations  13.6 us (2%)
    psum x4, blocking collectives, on_device(): lax.psum(shard_probability_share, ('dp', 'vocab'))  254 us
    all_gather x2, blocking collectives, merged(): pieces = jax.tree.map(lambda part: lax.all_gather(part, axis), value)  104 us
    psum x1, blocking collectives, on_device(): lax.psum(local_kept, ('dp', 'vocab'))  62.7 us
    all_gather x1, waiting for transfers between devices, on_device(): lax.all_gather(latent_vectors, 'dp', axis=0, tiled=True)  60 us
    reduce_sum x4, other arithmetic, nucleus_rows(): jnp.sum(prob * jax.nn.sigmoid((shifted - cutoffs[:, probe:probe + 1]) / s...  27.4 us
    dot_general x1, matrix products, on_device(): jnp.dot(lax.all_gather(latent_vectors, 'dp', axis=0, tiled=True), unembed...  20 us
    all_gather x1, blocking collectives, on_device(): lax.all_gather(softmax_divisor, 'dp', axis=0, tiled=True)  12.2 us
  transfers between devices with their start and end apart: 1, of which 1 were waited for; matrix products, arithmetic and copies ran while one was open for 0% of the time, Pallas kernels for 0%

commit v1 on v0

v1 whole, which is shorter than its diff:
```python
import functools

import jax
import jax.numpy as jnp
from jax import lax
from jax.experimental import pallas as pl
from jax.experimental.pallas import tpu as pltpu
from jax.sharding import PartitionSpec as P

MESH = pl.DeviceIdType.MESH
BISECT_PASSES = 4
PROBES = 4
soft_width = 0.25
sharpness = 0.02
initial_level = -16.0
first_spacing = 4.0

ROWS = 128
HALF = 512
STRIP = 144
NT = (((1,), (1,)), ((), ()))


def wait_bytes(ref, sem):
    pltpu.make_async_copy(ref, ref, sem).wait()


def places():
    dp, vo = lax.axis_index("dp"), lax.axis_index("vocab")
    plane = [(dp, lax.rem(vo + d, 16)) for d in range(1, 16)]
    column = [(lax.rem(dp + 2 * d, 8), vo) for d in range(1, 4)]
    sibling = (dp + 1 - 2 * lax.rem(dp, 2), vo)
    others = [(lax.rem(sibling[0] + 2 * d, 8), vo) for d in range(1, 4)]
    return dp, vo, plane, column, sibling, others


def send(src, dst, send_sem, recv_sem, device):
    copy = pltpu.make_async_remote_copy(
        src_ref=src, dst_ref=dst, send_sem=send_sem, recv_sem=recv_sem, device_id=device, device_id_type=MESH
    )
    copy.start()
    return copy


def fold(fn, init, vocab):
    whole = vocab // STRIP

    def step(t, carry):
        base = pl.multiple_of(t * STRIP, 8)
        for i in range(STRIP // 8):
            carry = fn(carry, pl.ds(base + 8 * i, 8))
        return carry

    return lax.fori_loop(0, whole, step, init)


def exchange(value, join, kind, index, plane, column, bufs, sems):
    out1, in1, out2, in2 = bufs
    send1, recv1, send2, recv2 = sems
    out1[kind, index] = value
    for d, device in enumerate(plane):
        send(out1.at[kind, index], in1.at[kind, index, d], send1.at[kind, index], recv1.at[kind, index], device)
    wait_bytes(in1.at[kind, index], recv1.at[kind, index])
    value = join([value] + [in1[kind, index, d] for d in range(15)])
    out2[kind, index] = value
    for d, device in enumerate(column):
        send(out2.at[kind, index], in2.at[kind, index, d], send2.at[kind, index], recv2.at[kind, index], device)
    wait_bytes(in2.at[kind, index], recv2.at[kind, index])
    return join([value] + [in2[kind, index, d] for d in range(3)])


def total_sum(parts):
    while len(parts) > 1:
        parts = [a + b for a, b in zip(parts[::2], parts[1::2])] + parts[len(parts) & ~1 :]
    return parts[0]


def joined_stats(parts):
    peak = functools.reduce(jnp.maximum, [p[0:1] for p in parts])
    summed = total_sum([p[1:2] * jnp.exp(0.5 * (p[0:1] - peak)) for p in parts])
    return jnp.concatenate([peak, summed], axis=0)


def kernel(
    x_ref, w_ref, div_ref, quota_ref, out_ref, scale_ref,
    xv, wv, logit, half, expo, rowinfo, final,
    so1, si1, so2, si2, mo1, mi1, mo2, mi2, ko1, ki1, ko2, ki2,
    load_sem, row_sem, half_sem, final_sem, s_sems, m_sems, k_sems,
):
    dp, vo, plane, column, sibling, others = places()
    core = lax.rem(dp, 2)
    vocab = w_ref.shape[0]
    depth = w_ref.shape[1]
    load_w = pltpu.make_async_copy(w_ref, wv, load_sem.at[0])
    load_w.start()
    load_x = pltpu.make_async_copy(x_ref, xv, load_sem.at[1])
    load_x.start()

    barrier = pltpu.get_barrier_semaphore()
    greeted = plane + column + [sibling] + others
    for device in greeted:
        pl.semaphore_signal(barrier, inc=1, device_id=device, device_id_type=MESH)
    rowinfo[dp] = jnp.concatenate([2.0 / div_ref[...], quota_ref[...].astype(jnp.float32) / 100.0], axis=0)
    pl.semaphore_wait(barrier, len(greeted))

    for device in column + [sibling] + others:
        send(rowinfo.at[dp], rowinfo.at[dp], row_sem.at[0], row_sem.at[1], device)

    load_w.wait()
    load_x.wait()
    logit[...] = jnp.zeros_like(logit)
    chunk = 1024

    def multiply(k, _):
        cols = pl.ds(pl.multiple_of(k * chunk, chunk), chunk)
        logit[...] += lax.dot_general(wv[:, cols], xv[:, cols], NT, preferred_element_type=jnp.float32)
        return 0

    lax.fori_loop(0, depth // chunk, multiply, 0)
    wait_bytes(rowinfo.at[pl.ds(0, 7)], row_sem.at[1])
    wait_bytes(rowinfo.at[pl.ds(0, 7)], row_sem.at[0])
    copies = []
    for j in range(4):
        block = 2 * j + 1 - core
        cols = pl.ds(pl.multiple_of(block * ROWS, ROWS), ROWS)
        logit[:, cols] = logit[:, cols] * rowinfo[block, 0:1]
        copies.append(
            send(logit.at[:, cols], half.at[1, :, pl.ds(j * ROWS, ROWS)], half_sem.at[0, j], half_sem.at[1, j], sibling)
        )
    level_parts = []
    for j in range(4):
        block = 2 * j + core
        cols = pl.ds(pl.multiple_of(block * ROWS, ROWS), ROWS)
        value = logit[:, cols] * rowinfo[block, 0:1]
        logit[:, cols] = value
        half[0, :, j * ROWS : (j + 1) * ROWS] = value
        level_parts.append(rowinfo[block, 1:2])
    level = jnp.concatenate(level_parts, axis=1)
    for copy in copies:
        copy.wait()

    tail = pl.ds(vocab // 8 * 8, vocab % 8)

    peak = jnp.full((8, HALF), -3e38, jnp.float32)
    for v in range(2):
        peak = fold(lambda c, r: jnp.maximum(c, half[v, r, :]), peak, vocab)
    peak = jnp.max(peak, axis=0, keepdims=True)
    for v in range(2):
        peak = jnp.maximum(peak, jnp.max(half[v, tail, :], axis=0, keepdims=True))
    own_sum = jnp.zeros((8, HALF), jnp.float32)
    wide = jnp.broadcast_to(peak, (8, HALF))
    tail_sum = jnp.zeros((1, HALF), jnp.float32)
    for v in range(2):

        def add_exp(carry, r):
            e = jnp.exp(0.5 * (half[v, r, :] - wide))
            expo[v, r, :] = e
            return carry + e

        own_sum = fold(add_exp, own_sum, vocab)
        e = jnp.exp(0.5 * (half[v, tail, :] - peak))
        expo[v, tail, :] = e
        tail_sum = tail_sum + jnp.sum(e, axis=0, keepdims=True)
    own_sum = jnp.sum(own_sum, axis=0, keepdims=True) + tail_sum
    stats = exchange(
        jnp.concatenate([peak, own_sum], axis=0), joined_stats, 0, 0, plane, column, (so1, si1, so2, si2), s_sems
    )
    top, total = stats[0:1], stats[1:2]
    share = 0.5 * jnp.exp(0.5 * (peak - top)) / total

    def masses(cuts):
        n = len(cuts)
        wides = [jnp.broadcast_to(c, (8, HALF)) for c in cuts]
        sums = tuple(jnp.zeros((8, HALF), jnp.float32) for _ in cuts)
        rest = [jnp.zeros((1, HALF), jnp.float32) for _ in cuts]
        for v in range(2):

            def add(carry, r):
                l, e = half[v, r, :], expo[v, r, :]
                return tuple(carry[k] + e * jnp.tanh(l - wides[k]) for k in range(n))

            sums = fold(add, sums, vocab)
            l, e = half[v, tail, :], expo[v, tail, :]
            rest = [rest[k] + jnp.sum(e * jnp.tanh(l - cuts[k]), axis=0, keepdims=True) for k in range(n)]
        return [share * (own_sum + jnp.sum(sums[k], axis=0, keepdims=True) + rest[k]) for k in range(n)]

    def bisect(r, carry):
        lower, spacing = carry
        parts = masses([top + 2.0 * (lower + spacing * (k + 1)) for k in range(PROBES)])
        mass = exchange(
            jnp.concatenate(parts, axis=0), total_sum, 0, r, plane, column, (mo1, mi1, mo2, mi2), m_sems
        )
        passed = jnp.sum(jax.nn.sigmoid((mass - level) / sharpness), axis=0, keepdims=True)
        estimate = lower + spacing * passed
        spacing = spacing / 2.0
        return estimate - spacing, spacing

    lower, spacing = lax.fori_loop(
        0, BISECT_PASSES, bisect, (jnp.full((1, HALF), initial_level, jnp.float32), jnp.float32(first_spacing))
    )
    cut = top + 2.0 * (lower + 2.0 * spacing)
    final[core, 0:1, :] = top
    final[core, 1:2, :] = cut
    kept = exchange(masses([cut])[0], total_sum, 0, 0, plane, column, (ko1, ki1, ko2, ki2), k_sems)
    final[core, 2:3, :] = 1.0 / (total * kept)
    swap = send(final.at[core], final.at[core], final_sem.at[0], final_sem.at[1], sibling)
    swap.wait()
    for block in range(8):
        h, j = block % 2, block // 2
        lanes = slice(j * ROWS, (j + 1) * ROWS)
        cols = slice(block * ROWS, (block + 1) * ROWS)
        top_b, cut_b, scale_b = (final[h, i : i + 1, lanes] for i in range(3))
        scale_ref[:, cols] = scale_b
        value = logit[:, cols]
        out_ref[:, cols] = jnp.exp(0.5 * (value - top_b)) * (0.5 + 0.5 * jnp.tanh(value - cut_b))

    for ins, sems, count in (((si1, si2), s_sems, 1), ((mi1, mi2), m_sems, BISECT_PASSES), ((ki1, ki2), k_sems, 1)):
        for index in range(count):
            wait_bytes(ins[0].at[0, index], sems[0].at[0, index])
            wait_bytes(ins[1].at[0, index], sems[2].at[0, index])


def slots(count, height):
    f32 = jnp.float32
    return [
        pltpu.VMEM((1, count, height, HALF), f32),
        pltpu.VMEM((1, count, 15, height, HALF), f32),
        pltpu.VMEM((1, count, height, HALF), f32),
        pltpu.VMEM((1, count, 3, height, HALF), f32),
    ]


def on_device(latent_vectors, unembedding_matrix, softmax_divisor, top_probability_quota):
    x = lax.all_gather(latent_vectors, "dp", axis=0, tiled=True)
    weights = unembedding_matrix.T
    vocab, depth = weights.shape
    batch = x.shape[0]
    f32 = jnp.float32
    dma = pltpu.SemaphoreType.DMA
    vmem = pl.BlockSpec(memory_space=pltpu.VMEM)
    hbm = pl.BlockSpec(memory_space=pl.ANY)
    out, scale = pl.pallas_call(
        kernel,
        out_shape=[jax.ShapeDtypeStruct((vocab, batch), f32), jax.ShapeDtypeStruct((1, batch), f32)],
        in_specs=[hbm, hbm, vmem, vmem],
        out_specs=[vmem, vmem],
        scratch_shapes=[
            pltpu.VMEM((batch, depth), jnp.bfloat16),
            pltpu.VMEM((vocab, depth), jnp.bfloat16),
            pltpu.VMEM((vocab, batch), f32),
            pltpu.VMEM((2, vocab, HALF), f32),
            pltpu.VMEM((2, vocab, HALF), f32),
            pltpu.VMEM((8, 2, ROWS), f32),
            pltpu.VMEM((2, 4, HALF), f32),
            *slots(1, 2),
            *slots(BISECT_PASSES, 4),
            *slots(1, 1),
            dma((2,)),
            dma((2,)),
            dma((2, 4)),
            dma((2,)),
            [dma((1, 1))] * 4,
            [dma((1, BISECT_PASSES))] * 4,
            [dma((1, 1))] * 4,
        ],
        compiler_params=pltpu.CompilerParams(
            collective_id=0, has_side_effects=True, vmem_limit_bytes=58 * 1024 * 1024
        ),
        cost_estimate=pl.CostEstimate(
            flops=2 * vocab * depth * batch, bytes_accessed=2 * depth * (vocab + batch), transcendentals=20 * vocab * batch
        ),
    )(x, weights, softmax_divisor[None, :], top_probability_quota[None, :])
    return (out * scale).T


def solution(mesh):
    placed = (P("dp", None), P(None, ("dp", "vocab")), P("dp"), P("dp"))
    return jax.shard_map(
        on_device, mesh=mesh, in_specs=placed, out_specs=P(None, ("dp", "vocab")), check_vma=False
    )
```

time: 585 us -> 201 us (0.34)
  blocking collectives: 441 us -> 0 us
  Pallas kernels: 0 us -> 99.9 us
  other arithmetic: 40.2 us -> 4.76 us
  waiting for transfers between devices: 60.7 us -> 82.3 us
  matrix products: 20 us -> 0 us
    psum x5 -> x0, blocking collectives: 317 us -> none  [the longest x4 254 us: on_device(): lax.psum(shard_probability_share, ('dp', 'vocab'))]
    all_gather x4 -> x0, blocking collectives: 124 us -> none  [the longest x2 104 us: merged(): pieces = jax.tree.map(lambda part: lax.all_gather(part, axis), value)]
    pallas_call x0 -> x1, Pallas kernels: none -> 99.9 us  [on_device(): pl.pallas_call(kernel, out_shape=[jax.ShapeDtypeStruct((vocab, batch), f3...]
    reduce_sum x10 -> x0, other arithmetic: 32.7 us -> none  [the longest x4 27.4 us: nucleus_rows(): jnp.sum(prob * jax.nn.sigmoid((shifted - cutoffs[:, probe:probe + 1]) / s...]
    all_gather x1, waiting for transfers between devices: 60 us -> 81.6 us  [on_device(): x = lax.all_gather(latent_vectors, 'dp', axis=0, tiled=True)]
    dot_general x1 -> x0, matrix products: 20 us -> none  [on_device(): jnp.dot(lax.all_gather(latent_vectors, 'dp', axis=0, tiled=True), unembed...]
where the time goes in v1:
time: 201 us; the launch traced here: 200 us
  Pallas kernels  99.9 us (50%)
  waiting for transfers between devices  82.3 us (41%)
  between operations  13.4 us (7%)
  other arithmetic  4.76 us (2%)
    pallas_call x1, Pallas kernels, on_device(): pl.pallas_call(kernel, out_shape=[jax.ShapeDtypeStruct((vocab, batch), f3...  99.9 us
    all_gather x1, waiting for transfers between devices, on_device(): x = lax.all_gather(latent_vectors, 'dp', axis=0, tiled=True)  81.6 us
    transpose x1, other arithmetic, on_device(): return (out * scale).T  4.76 us
  transfers between devices with their start and end apart: 1, of which 1 were waited for; matrix products, arithmetic and copies ran while one was open for 0% of the time, Pallas kernels for 0%

profile of v1, /device:TPU:1, one launch (start us, length us, event | category | flops | bytes accessed | tf_op | source)
XLA Modules:
  0.0 200.4 jit_solution(2768584849703983182)
XLA Ops:
  6.5 0.0 all-gather.2.cloned.1.call-start
  6.5 0.7 all-gather.2.cloned.1.call-update
  7.3 81.6 %all-gather.2.cloned.1.call-done.x_ref = bf16[1024,7168]{1,0:T(8,128)(2,1)} async-done(((bf16[128,7168]{1,0:T(8,128)(2,1)}), bf16[1024,7168]{1,0:T(8,128)(2,1)}) %all-gather.2.cloned.1.call-update) | async-done | bytes 14680080 | tf_op jit(solution)/shard_map/all_gather | solution.py:234
  88.9 99.9 %shard_map.46 = (f32[1010,1024]{1,0:T(8,128)}, f32[1,1024]{1,0:T(1,128)}) custom-call(bf16[1024,7168]{1,0:T(8,128)(2,1)} %all-gather.2.cloned.1.call-done.x_ref, bf16[1010,7168]{1,0:T(8,128)(2,1)} %bitcast.7, f32[1,128]{1,0:T(1,128)} %bitcast.8, s32[1,128]{1,0:T(1,128)} %bitcast.9), custom_call_target="tpu_custom_call" | custom-call | flops 14826864640 | bytes 29159424 | tf_op jit(solution)/shard_map/pallas_call | solution.py:242
  188.8 4.8 %multiply_bitcast_fusion = f32[1024,1010]{0,1:T(8,128)} fusion(f32[1010,1024]{1,0:T(8,128)} %get-tuple-element.7, f32[1024]{0:T(1024)} %bitcast.6), kind=kLoop, calls=%fused_computation | loop fusion | flops 1034240 | bytes 8278016 | tf_op jit(solution)/shard_map/transpose | solution.py:273
Async XLA Ops:
  6.5 82.3 %all-gather.2.cloned.1.call-start = ((), (), s32[]{:S(2)}) async-start(), calls=%async_computation | async-start | bytes 16515072 | tf_op jit(solution)/shard_map/all_gather | solution.py:234
Sparse Core Ops, SparseCore 0:
  9.0 79.7 all-gather.1

commit v2 on v1

--- a/solution.py
+++ b/solution.py
@@ -18,6 +18,10 @@
 ROWS = 128
 HALF = 512
 STRIP = 144
+CHUNKS = 7
+UNITS = 4 * CHUNKS
+LAG_SHARE = 4
+LAG_MULTIPLY = 6
 NT = (((1,), (1,)), ((), ()))
 
 
@@ -85,16 +89,20 @@
     x_ref, w_ref, div_ref, quota_ref, out_ref, scale_ref,
     xv, wv, logit, half, expo, rowinfo, final,
     so1, si1, so2, si2, mo1, mi1, mo2, mi2, ko1, ki1, ko2, ki2,
-    load_sem, row_sem, half_sem, final_sem, s_sems, m_sems, k_sems,
+    load_sem, row_sem, y_sem, p_sem, c_sem, half_sem, final_sem, s_sems, m_sems, k_sems,
 ):
     dp, vo, plane, column, sibling, others = places()
     core = lax.rem(dp, 2)
     vocab = w_ref.shape[0]
     depth = w_ref.shape[1]
-    load_w = pltpu.make_async_copy(w_ref, wv, load_sem.at[0])
-    load_w.start()
-    load_x = pltpu.make_async_copy(x_ref, xv, load_sem.at[1])
+    chunk = depth // CHUNKS
+    load_x = pltpu.make_async_copy(x_ref, xv.at[pl.ds(pl.multiple_of(dp * ROWS, ROWS), ROWS)], load_sem.at[CHUNKS])
     load_x.start()
+    load_w = []
+    for k in range(CHUNKS):
+        cols = pl.ds(k * chunk, chunk)
+        load_w.append(pltpu.make_async_copy(w_ref.at[:, cols], wv.at[:, cols], load_sem.at[k]))
+        load_w[k].start()
 
     barrier = pltpu.get_barrier_semaphore()
     greeted = plane + column + [sibling] + others
@@ -106,38 +114,101 @@
     for device in column + [sibling] + others:
         send(rowinfo.at[dp], rowinfo.at[dp], row_sem.at[0], row_sem.at[1], device)
 
-    load_w.wait()
+    x_at, z_at = lax.div(vo, 4), lax.rem(vo, 4)
+    y_at = lax.div(dp, 2)
+    line_z = [(dp, x_at * 4 + lax.rem(z_at + e, 4)) for e in range(1, 4)]
+    line_x = [(dp, lax.rem(x_at + e, 4) * 4 + z_at) for e in range(1, 4)]
+    first_row = pl.multiple_of(dp * ROWS, ROWS)
+
+    def unit(m):
+        i = m - CHUNKS
+        near = i < 2 * CHUNKS
+        offset = jnp.where(i < 0, 0, jnp.where(near, 1 + 2 * lax.rem(i, 2), 2))
+        k = jnp.where(i < 0, m, jnp.where(near, lax.div(i, 2), i - 2 * CHUNKS))
+        return offset, pl.ds(pl.multiple_of(k * chunk, chunk), chunk), k
+
+    def pieces(block):
+        base = block * ROWS
+        return (
+            pl.ds(pl.multiple_of(base + 16 * z_at, 16), 16),
+            pl.ds(pl.multiple_of(base + 64 + 16 * x_at, 16), 16),
+        )
+
+    def spread(m, _):
+        offset, cols, _ = unit(m)
+        target = (lax.rem(2 * (y_at + 4 - offset) + core, 8), vo)
+        for local, there in zip(pieces(0), pieces(dp)):
+            send(x_ref.at[local, cols], xv.at[there, cols], y_sem.at[0, m], y_sem.at[1, m], target)
+        return 0
+
+    def share_own(m, _):
+        _, cols, _ = unit(m)
+        send(x_ref.at[:, cols], xv.at[pl.ds(first_row, ROWS), cols], c_sem.at[0, m], c_sem.at[1, m], sibling)
+        return 0
+
+    def source_block(offset):
+        return lax.rem(2 * (y_at + offset) + core, 8)
+
+    def pass_on(m):
+        offset, cols, _ = unit(m)
+        wait_bytes(xv.at[pl.ds(0, 32), cols], y_sem.at[1, m])
+        for rows, line in zip(pieces(source_block(offset)), (line_z, line_x)):
+            for device in line:
+                send(xv.at[rows, cols], xv.at[rows, cols], p_sem.at[0, m], p_sem.at[1, m], device)
+
+    def share(m):
+        offset, cols, _ = unit(m)
+        wait_bytes(xv.at[pl.ds(0, 96), cols], p_sem.at[1, m])
+        rows = pl.ds(pl.multiple_of(source_block(offset) * ROWS, ROWS), ROWS)
+        send(xv.at[rows, cols], xv.at[rows, cols], c_sem.at[0, m], c_sem.at[1, m], sibling)
+
+    def multiply(m):
+        offset, cols, k = unit(m)
+        plane_at = lax.rem(y_at + offset, 4)
+        rows = pl.ds(pl.multiple_of(plane_at * 2 * ROWS, 2 * ROWS), 2 * ROWS)
+        wait_bytes(xv.at[pl.ds(0, ROWS), cols], c_sem.at[1, m])
+        logit[:, rows] += lax.dot_general(wv[:, cols], xv[rows, cols], NT, preferred_element_type=jnp.float32)
+
+        @pl.when(k == CHUNKS - 1)
+        def _():
+            block = 2 * plane_at + 1 - core
+            cols = pl.ds(pl.multiple_of(block * ROWS, ROWS), ROWS)
+            there = pl.ds(pl.multiple_of(plane_at * ROWS, ROWS), ROWS)
+            logit[:, cols] = logit[:, cols] * rowinfo[block, 0:1]
+            send(logit.at[:, cols], half.at[1, :, there], half_sem.at[0, plane_at], half_sem.at[1, plane_at], sibling)
+            block = 2 * plane_at + core
+            cols = pl.ds(pl.multiple_of(block * ROWS, ROWS), ROWS)
+            value = logit[:, cols] * rowinfo[block, 0:1]
+            logit[:, cols] = value
+            half[0, :, there] = value
+
+    lax.fori_loop(0, CHUNKS, share_own, 0)
+    lax.fori_loop(CHUNKS, UNITS, spread, 0)
+    logit[...] = jnp.zeros_like(logit)
     load_x.wait()
-    logit[...] = jnp.zeros_like(logit)
-    chunk = 1024
-
-    def multiply(k, _):
-        cols = pl.ds(pl.multiple_of(k * chunk, chunk), chunk)
-        logit[...] += lax.dot_general(wv[:, cols], xv[:, cols], NT, preferred_element_type=jnp.float32)
-        return 0
-
-    lax.fori_loop(0, depth // chunk, multiply, 0)
+    for m in range(CHUNKS):
+        load_w[m].wait()
+        if m < CHUNKS - LAG_MULTIPLY:
+            multiply(m)
     wait_bytes(rowinfo.at[pl.ds(0, 7)], row_sem.at[1])
     wait_bytes(rowinfo.at[pl.ds(0, 7)], row_sem.at[0])
-    copies = []
+
+    def step(t, _):
+        @pl.when(t < UNITS)
+        def _():
+            pass_on(t)
+
+        @pl.when((t >= CHUNKS + LAG_SHARE) & (t < UNITS + LAG_SHARE))
+        def _():
+            share(t - LAG_SHARE)
+
+        multiply(t - LAG_MULTIPLY)
+        return 0
+
+    lax.fori_loop(CHUNKS, UNITS + LAG_MULTIPLY, step, 0)
+    level = jnp.concatenate([rowinfo[2 * j + core, 1:2] for j in range(4)], axis=1)
     for j in range(4):
-        block = 2 * j + 1 - core
-        cols = pl.ds(pl.multiple_of(block * ROWS, ROWS), ROWS)
-        logit[:, cols] = logit[:, cols] * rowinfo[block, 0:1]
-        copies.append(
-            send(logit.at[:, cols], half.at[1, :, pl.ds(j * ROWS, ROWS)], half_sem.at[0, j], half_sem.at[1, j], sibling)
-        )
-    level_parts = []
-    for j in range(4):
-        block = 2 * j + core
-        cols = pl.ds(pl.multiple_of(block * ROWS, ROWS), ROWS)
-        value = logit[:, cols] * rowinfo[block, 0:1]
-        logit[:, cols] = value
-        half[0, :, j * ROWS : (j + 1) * ROWS] = value
-        level_parts.append(rowinfo[block, 1:2])
-    level = jnp.concatenate(level_parts, axis=1)
-    for copy in copies:
-        copy.wait()
+        wait_bytes(half.at[1, :, pl.ds(0, ROWS)], half_sem.at[1, j])
 
     tail = pl.ds(vocab // 8 * 8, vocab % 8)
 
@@ -214,6 +285,20 @@
         value = logit[:, cols]
         out_ref[:, cols] = jnp.exp(0.5 * (value - top_b)) * (0.5 + 0.5 * jnp.tanh(value - cut_b))
 
+    def left(m, _):
+        cols = pl.ds(0, chunk)
+        wait_bytes(xv.at[pl.ds(0, ROWS), cols], c_sem.at[0, m])
+
+        @pl.when(m >= CHUNKS)
+        def _():
+            wait_bytes(xv.at[pl.ds(0, 32), cols], y_sem.at[0, m])
+            wait_bytes(xv.at[pl.ds(0, 96), cols], p_sem.at[0, m])
+
+        return 0
+
+    lax.fori_loop(0, UNITS, left, 0)
+    for j in range(4):
+        wait_bytes(half.at[1, :, pl.ds(0, ROWS)], half_sem.at[0, j])
     for ins, sems, count in (((si1, si2), s_sems, 1), ((mi1, mi2), m_sems, BISECT_PASSES), ((ki1, ki2), k_sems, 1)):
         for index in range(count):
             wait_bytes(ins[0].at[0, index], sems[0].at[0, index])
@@ -231,10 +316,9 @@
 
 
 def on_device(latent_vectors, unembedding_matrix, softmax_divisor, top_probability_quota):
-    x = lax.all_gather(latent_vectors, "dp", axis=0, tiled=True)
     weights = unembedding_matrix.T
     vocab, depth = weights.shape
-    batch = x.shape[0]
+    batch = 8 * ROWS
     f32 = jnp.float32
     dma = pltpu.SemaphoreType.DMA
     vmem = pl.BlockSpec(memory_space=pltpu.VMEM)
@@ -255,8 +339,11 @@
             *slots(1, 2),
             *slots(BISECT_PASSES, 4),
             *slots(1, 1),
+            dma((CHUNKS + 1,)),
             dma((2,)),
-            dma((2,)),
+            dma((2, UNITS)),
+            dma((2, UNITS)),
+            dma((2, UNITS)),
             dma((2, 4)),
             dma((2,)),
             [dma((1, 1))] * 4,
@@ -269,7 +356,7 @@
         cost_estimate=pl.CostEstimate(
             flops=2 * vocab * depth * batch, bytes_accessed=2 * depth * (vocab + batch), transcendentals=20 * vocab * batch
         ),
-    )(x, weights, softmax_divisor[None, :], top_probability_quota[None, :])
+    )(latent_vectors, weights, softmax_divisor[None, :], top_probability_quota[None, :])
     return (out * scale).T
 
 

time: 201 us -> 123 us (0.61)
  waiting for transfers between devices: 82.3 us -> 0 us
  Pallas kernels: 99.9 us -> 118 us
  between operations: 13.4 us -> 0.01 us
    all_gather x1 -> x0, waiting for transfers between devices: 81.6 us -> none  [on_device(): x = lax.all_gather(latent_vectors, 'dp', axis=0, tiled=True)]
    pallas_call x1, Pallas kernels: 99.9 us -> 118 us  [on_device(): pl.pallas_call(kernel, out_shape=[jax.ShapeDtypeStruct((vocab, batch), f3...]
  transfers between devices with their start and end apart: 1 -> 0, of which waited for: 1 -> 0; matrix products, arithmetic and copies ran while one was open for 0% -> 0% of each run, Pallas kernels for 0% -> 0%
where the time goes in v2:
time: 123 us
  Pallas kernels  118 us (96%)
  other arithmetic  4.76 us (4%)
    pallas_call x1, Pallas kernels, on_device(): pl.pallas_call(kernel, out_shape=[jax.ShapeDtypeStruct((vocab, batch), f3...  118 us
    transpose x1, other arithmetic, on_device(): return (out * scale).T  4.76 us

profile of v2, /device:TPU:1, one launch (start us, length us, event | category | flops | bytes accessed | tf_op | source)
XLA Modules:
  0.0 123.0 jit_solution(2055945145453351082)
XLA Ops:
  0.0 118.2 %shard_map.46 = (f32[1010,1024]{1,0:T(8,128)}, f32[1,1024]{1,0:T(1,128)}) custom-call(bf16[128,7168]{1,0:T(8,128)(2,1)} %x_ref.1, bf16[1010,7168]{1,0:T(8,128)(2,1)} %bitcast.7, f32[1,128]{1,0:T(1,128)} %bitcast.8, s32[1,128]{1,0:T(1,128)} %bitcast.9), custom_call_target="tpu_custom_call" | custom-call | flops 14826864640 | bytes 29159424 | tf_op jit(solution)/shard_map/pallas_call | solution.py:326
  118.2 4.8 %multiply_bitcast_fusion = f32[1024,1010]{0,1:T(8,128)} fusion(f32[1010,1024]{1,0:T(8,128)} %get-tuple-element.7, f32[1024]{0:T(1024)} %bitcast.6), kind=kLoop, calls=%fused_computation | loop fusion | flops 1034240 | bytes 8278016 | tf_op jit(solution)/shard_map/transpose | solution.py:360

commit v3 on v2

--- a/solution.py
+++ b/solution.py
@@ -17,11 +17,15 @@
 
 ROWS = 128
 HALF = 512
-STRIP = 144
+GROUP = 256
+GROUPS = 2
+STRIP = 336
 CHUNKS = 7
 UNITS = 4 * CHUNKS
-LAG_SHARE = 4
-LAG_MULTIPLY = 6
+LAG_FORWARD = 3
+LAG_SHARE = 6
+LAG_MULTIPLY = 8
+EARLY = 4
 NT = (((1,), (1,)), ((), ()))
 
 
@@ -47,30 +51,29 @@
 
 
 def fold(fn, init, vocab):
-    whole = vocab // STRIP
-
     def step(t, carry):
         base = pl.multiple_of(t * STRIP, 8)
         for i in range(STRIP // 8):
             carry = fn(carry, pl.ds(base + 8 * i, 8))
         return carry
 
-    return lax.fori_loop(0, whole, step, init)
-
-
-def exchange(value, join, kind, index, plane, column, bufs, sems):
+    return lax.fori_loop(0, vocab // STRIP, step, init)
+
+
+def exchange(value, join, trip, plane, column, bufs, sems):
     out1, in1, out2, in2 = bufs
-    send1, recv1, send2, recv2 = sems
-    out1[kind, index] = value
+    out1[trip] = value
     for d, device in enumerate(plane):
-        send(out1.at[kind, index], in1.at[kind, index, d], send1.at[kind, index], recv1.at[kind, index], device)
-    wait_bytes(in1.at[kind, index], recv1.at[kind, index])
-    value = join([value] + [in1[kind, index, d] for d in range(15)])
-    out2[kind, index] = value
+        send(out1.at[trip], in1.at[trip, d], sems.at[0, trip], sems.at[1, trip], device)
+    yield
+    wait_bytes(in1.at[trip], sems.at[1, trip])
+    value = join([value] + [in1[trip, d] for d in range(15)])
+    out2[trip] = value
     for d, device in enumerate(column):
-        send(out2.at[kind, index], in2.at[kind, index, d], send2.at[kind, index], recv2.at[kind, index], device)
-    wait_bytes(in2.at[kind, index], recv2.at[kind, index])
-    return join([value] + [in2[kind, index, d] for d in range(3)])
+        send(out2.at[trip], in2.at[trip, d], sems.at[2, trip], sems.at[3, trip], device)
+    yield
+    wait_bytes(in2.at[trip], sems.at[3, trip])
+    return join([value] + [in2[trip, d] for d in range(3)])
 
 
 def total_sum(parts):
@@ -87,9 +90,9 @@
 
 def kernel(
     x_ref, w_ref, div_ref, quota_ref, out_ref, scale_ref,
-    xv, wv, logit, half, expo, rowinfo, final,
-    so1, si1, so2, si2, mo1, mi1, mo2, mi2, ko1, ki1, ko2, ki2,
-    load_sem, row_sem, y_sem, p_sem, c_sem, half_sem, final_sem, s_sems, m_sems, k_sems,
+    xv, wv, logit, half, expo, rowinfo, final, scale,
+    stat_bufs, mass_bufs, kept_bufs,
+    load_sem, row_sem, y_sem, p_sem, f_sem, c_sem, half_sem, final_sem, stat_sem, mass_sem, kept_sem,
 ):
     dp, vo, plane, column, sibling, others = places()
     core = lax.rem(dp, 2)
@@ -153,12 +156,22 @@
         offset, cols, _ = unit(m)
         wait_bytes(xv.at[pl.ds(0, 32), cols], y_sem.at[1, m])
         for rows, line in zip(pieces(source_block(offset)), (line_z, line_x)):
-            for device in line:
+            for device in (line[0], line[2]):
                 send(xv.at[rows, cols], xv.at[rows, cols], p_sem.at[0, m], p_sem.at[1, m], device)
+
+    def forward(m):
+        offset, cols, k = unit(m)
+        wait_bytes(xv.at[pl.ds(0, 64), cols], p_sem.at[1, m])
+        base = source_block(offset) * ROWS
+        for at, shift, line in ((z_at, 0, line_z), (x_at, 64, line_x)):
+            for part, (step, device) in enumerate(((3, line[0]), (1, line[2]))):
+                rows = pl.ds(pl.multiple_of(base + shift + 16 * lax.rem(at + step, 4), 16), 16)
+                cols = pl.ds(pl.multiple_of(k * chunk + part * (chunk // 2), chunk // 2), chunk // 2)
+                send(xv.at[rows, cols], xv.at[rows, cols], f_sem.at[0, m], f_sem.at[1, m], device)
 
     def share(m):
         offset, cols, _ = unit(m)
-        wait_bytes(xv.at[pl.ds(0, 96), cols], p_sem.at[1, m])
+        wait_bytes(xv.at[pl.ds(0, 32), cols], f_sem.at[1, m])
         rows = pl.ds(pl.multiple_of(source_block(offset) * ROWS, ROWS), ROWS)
         send(xv.at[rows, cols], xv.at[rows, cols], c_sem.at[0, m], c_sem.at[1, m], sibling)
 
@@ -186,10 +199,9 @@
     lax.fori_loop(CHUNKS, UNITS, spread, 0)
     logit[...] = jnp.zeros_like(logit)
     load_x.wait()
-    for m in range(CHUNKS):
+    for m in range(EARLY):
         load_w[m].wait()
-        if m < CHUNKS - LAG_MULTIPLY:
-            multiply(m)
+        multiply(m)
     wait_bytes(rowinfo.at[pl.ds(0, 7)], row_sem.at[1])
     wait_bytes(rowinfo.at[pl.ds(0, 7)], row_sem.at[0])
 
@@ -198,11 +210,24 @@
         def _():
             pass_on(t)
 
+        @pl.when((t >= CHUNKS + LAG_FORWARD) & (t < UNITS + LAG_FORWARD))
+        def _():
+            forward(t - LAG_FORWARD)
+
         @pl.when((t >= CHUNKS + LAG_SHARE) & (t < UNITS + LAG_SHARE))
         def _():
             share(t - LAG_SHARE)
 
-        multiply(t - LAG_MULTIPLY)
+        m = t - LAG_MULTIPLY
+
+        @pl.when((m >= EARLY) & (m < CHUNKS))
+        def _():
+            wait_bytes(wv.at[:, pl.ds(0, chunk)], load_sem.at[m])
+
+        @pl.when(m >= EARLY)
+        def _():
+            multiply(m)
+
         return 0
 
     lax.fori_loop(CHUNKS, UNITS + LAG_MULTIPLY, step, 0)
@@ -212,78 +237,100 @@
 
     tail = pl.ds(vocab // 8 * 8, vocab % 8)
 
-    peak = jnp.full((8, HALF), -3e38, jnp.float32)
-    for v in range(2):
-        peak = fold(lambda c, r: jnp.maximum(c, half[v, r, :]), peak, vocab)
-    peak = jnp.max(peak, axis=0, keepdims=True)
-    for v in range(2):
-        peak = jnp.maximum(peak, jnp.max(half[v, tail, :], axis=0, keepdims=True))
-    own_sum = jnp.zeros((8, HALF), jnp.float32)
-    wide = jnp.broadcast_to(peak, (8, HALF))
-    tail_sum = jnp.zeros((1, HALF), jnp.float32)
-    for v in range(2):
-
-        def add_exp(carry, r):
-            e = jnp.exp(0.5 * (half[v, r, :] - wide))
-            expo[v, r, :] = e
-            return carry + e
-
-        own_sum = fold(add_exp, own_sum, vocab)
-        e = jnp.exp(0.5 * (half[v, tail, :] - peak))
-        expo[v, tail, :] = e
-        tail_sum = tail_sum + jnp.sum(e, axis=0, keepdims=True)
-    own_sum = jnp.sum(own_sum, axis=0, keepdims=True) + tail_sum
-    stats = exchange(
-        jnp.concatenate([peak, own_sum], axis=0), joined_stats, 0, 0, plane, column, (so1, si1, so2, si2), s_sems
-    )
-    top, total = stats[0:1], stats[1:2]
-    share = 0.5 * jnp.exp(0.5 * (peak - top)) / total
-
-    def masses(cuts):
-        n = len(cuts)
-        wides = [jnp.broadcast_to(c, (8, HALF)) for c in cuts]
-        sums = tuple(jnp.zeros((8, HALF), jnp.float32) for _ in cuts)
-        rest = [jnp.zeros((1, HALF), jnp.float32) for _ in cuts]
+    def follow(g):
+        lanes = slice(g * GROUP, (g + 1) * GROUP)
+
+        peak = jnp.full((8, GROUP), -3e38, jnp.float32)
         for v in range(2):
-
-            def add(carry, r):
-                l, e = half[v, r, :], expo[v, r, :]
-                return tuple(carry[k] + e * jnp.tanh(l - wides[k]) for k in range(n))
-
-            sums = fold(add, sums, vocab)
-            l, e = half[v, tail, :], expo[v, tail, :]
-            rest = [rest[k] + jnp.sum(e * jnp.tanh(l - cuts[k]), axis=0, keepdims=True) for k in range(n)]
-        return [share * (own_sum + jnp.sum(sums[k], axis=0, keepdims=True) + rest[k]) for k in range(n)]
-
-    def bisect(r, carry):
-        lower, spacing = carry
-        parts = masses([top + 2.0 * (lower + spacing * (k + 1)) for k in range(PROBES)])
-        mass = exchange(
-            jnp.concatenate(parts, axis=0), total_sum, 0, r, plane, column, (mo1, mi1, mo2, mi2), m_sems
+            peak = fold(lambda c, r: jnp.maximum(c, half[v, r, lanes]), peak, vocab)
+        peak = jnp.max(peak, axis=0, keepdims=True)
+        for v in range(2):
+            peak = jnp.maximum(peak, jnp.max(half[v, tail, lanes], axis=0, keepdims=True))
+        own_sum = jnp.zeros((8, GROUP), jnp.float32)
+        wide = jnp.broadcast_to(peak, (8, GROUP))
+        tail_sum = jnp.zeros((1, GROUP), jnp.float32)
+        for v in range(2):
+
+            def add_exp(carry, r):
+                e = jnp.exp(0.5 * (half[v, r, lanes] - wide))
+                expo[v, r, lanes] = e
+                return carry + e
+
+            own_sum = fold(add_exp, own_sum, vocab)
+            e = jnp.exp(0.5 * (half[v, tail, lanes] - peak))
+            expo[v, tail, lanes] = e
+            tail_sum = tail_sum + jnp.sum(e, axis=0, keepdims=True)
+        own_sum = jnp.sum(own_sum, axis=0, keepdims=True) + tail_sum
+        stats = yield from exchange(
+            jnp.concatenate([peak, own_sum], axis=0), joined_stats, g, plane, column, stat_bufs, stat_sem
         )
-        passed = jnp.sum(jax.nn.sigmoid((mass - level) / sharpness), axis=0, keepdims=True)
-        estimate = lower + spacing * passed
-        spacing = spacing / 2.0
-        return estimate - spacing, spacing
-
-    lower, spacing = lax.fori_loop(
-        0, BISECT_PASSES, bisect, (jnp.full((1, HALF), initial_level, jnp.float32), jnp.float32(first_spacing))
-    )
-    cut = top + 2.0 * (lower + 2.0 * spacing)
-    final[core, 0:1, :] = top
-    final[core, 1:2, :] = cut
-    kept = exchange(masses([cut])[0], total_sum, 0, 0, plane, column, (ko1, ki1, ko2, ki2), k_sems)
-    final[core, 2:3, :] = 1.0 / (total * kept)
-    swap = send(final.at[core], final.at[core], final_sem.at[0], final_sem.at[1], sibling)
+        top, total = stats[0:1], stats[1:2]
+        share = 0.5 * jnp.exp(0.5 * (peak - top)) / total
+
+        def masses(cuts):
+            n = len(cuts)
+            wides = [jnp.broadcast_to(c, (8, GROUP)) for c in cuts]
+            sums = tuple(jnp.zeros((8, GROUP), jnp.float32) for _ in cuts)
+            rest = [jnp.zeros((1, GROUP), jnp.float32) for _ in cuts]
+            for v in range(2):
+
+                def add(carry, r):
+                    l, e = half[v, r, lanes], expo[v, r, lanes]
+                    return tuple(carry[k] + e * jnp.tanh(l - wides[k]) for k in range(n))
+
+                sums = fold(add, sums, vocab)
+                l, e = half[v, tail, lanes], expo[v, tail, lanes]
+                rest = [rest[k] + jnp.sum(e * jnp.tanh(l - cuts[k]), axis=0, keepdims=True) for k in range(n)]
+            parts = [share * (own_sum + jnp.sum(sums[k], axis=0, keepdims=True) + rest[k]) for k in range(n)]
+            return jnp.concatenate(parts, axis=0)
+
+        lower, spacing = jnp.full((1, GROUP), initial_level, jnp.float32), first_spacing
+        for r in range(BISECT_PASSES):
+            parts = masses([top + 2.0 * (lower + spacing * (k + 1)) for k in range(PROBES)])
+            mass = yield from exchange(
+                parts, total_sum, r * GROUPS + g, plane, column, mass_bufs, mass_sem
+            )
+            passed = jnp.sum(jax.nn.sigmoid((mass - level[:, lanes]) / sharpness), axis=0, keepdims=True)
+            estimate = lower + spacing * passed
+            spacing = spacing / 2.0
+            lower = estimate - spacing
+        cut = top + 2.0 * (lower + 2.0 * spacing)
+        final[core, 0:1, lanes] = top
+        final[core, 1:2, lanes] = cut
+        here = final.at[core, :, pl.ds(g * GROUP, GROUP)]
+        send(here, here, final_sem.at[0, g], final_sem.at[1, g], sibling)
+        kept = yield from exchange(masses([cut]), total_sum, g, plane, column, kept_bufs, kept_sem)
+        scale[core, 0:1, lanes] = 1.0 / (total * kept)
+
+    def weigh(h, g):
+        for j in (2 * g, 2 * g + 1):
+            lanes = slice(j * ROWS, (j + 1) * ROWS)
+            cols = pl.ds(pl.multiple_of((2 * j + h) * ROWS, ROWS), ROWS)
+            top, cut = final[h, 0:1, lanes], final[h, 1:2, lanes]
+            value = logit[:, cols]
+            out_ref[:, cols] = jnp.exp(0.5 * (value - top)) * (0.5 + 0.5 * jnp.tanh(value - cut))
+
+    rows_of = [follow(g) for g in range(GROUPS)]
+    for _ in range(BISECT_PASSES + 1):
+        for part in range(2):
+            for rows in rows_of:
+                next(rows)
+    for rows in rows_of:
+        next(rows)
+    for g in range(GROUPS):
+        weigh(core, g)
+    for g in range(GROUPS):
+        wait_bytes(final.at[core, :, pl.ds(g * GROUP, GROUP)], final_sem.at[1, g])
+        weigh(1 - core, g)
+    for rows in rows_of:
+        next(rows)
+    for rows in rows_of:
+        next(rows, None)
+    swap = send(scale.at[core], scale.at[core], final_sem.at[0, GROUPS], final_sem.at[1, GROUPS], sibling)
     swap.wait()
     for block in range(8):
-        h, j = block % 2, block // 2
-        lanes = slice(j * ROWS, (j + 1) * ROWS)
-        cols = slice(block * ROWS, (block + 1) * ROWS)
-        top_b, cut_b, scale_b = (final[h, i : i + 1, lanes] for i in range(3))
-        scale_ref[:, cols] = scale_b
-        value = logit[:, cols]
-        out_ref[:, cols] = jnp.exp(0.5 * (value - top_b)) * (0.5 + 0.5 * jnp.tanh(value - cut_b))
+        lanes = slice(block // 2 * ROWS, (block // 2 + 1) * ROWS)
+        scale_ref[:, block * ROWS : (block + 1) * ROWS] = scale[block % 2, :, lanes]
 
     def left(m, _):
         cols = pl.ds(0, chunk)
@@ -292,26 +339,29 @@
         @pl.when(m >= CHUNKS)
         def _():
             wait_bytes(xv.at[pl.ds(0, 32), cols], y_sem.at[0, m])
-            wait_bytes(xv.at[pl.ds(0, 96), cols], p_sem.at[0, m])
+            wait_bytes(xv.at[pl.ds(0, 64), cols], p_sem.at[0, m])
+            wait_bytes(xv.at[pl.ds(0, 32), cols], f_sem.at[0, m])
 
         return 0
 
     lax.fori_loop(0, UNITS, left, 0)
     for j in range(4):
         wait_bytes(half.at[1, :, pl.ds(0, ROWS)], half_sem.at[0, j])
-    for ins, sems, count in (((si1, si2), s_sems, 1), ((mi1, mi2), m_sems, BISECT_PASSES), ((ki1, ki2), k_sems, 1)):
-        for index in range(count):
-            wait_bytes(ins[0].at[0, index], sems[0].at[0, index])
-            wait_bytes(ins[1].at[0, index], sems[2].at[0, index])
+    for g in range(GROUPS):
+        wait_bytes(final.at[core, :, pl.ds(g * GROUP, GROUP)], final_sem.at[0, g])
+    for (_, in1, _, in2), sems in ((stat_bufs, stat_sem), (mass_bufs, mass_sem), (kept_bufs, kept_sem)):
+        for trip in range(in1.shape[0]):
+            wait_bytes(in1.at[trip], sems.at[0, trip])
+            wait_bytes(in2.at[trip], sems.at[2, trip])
 
 
 def slots(count, height):
     f32 = jnp.float32
     return [
-        pltpu.VMEM((1, count, height, HALF), f32),
-        pltpu.VMEM((1, count, 15, height, HALF), f32),
-        pltpu.VMEM((1, count, height, HALF), f32),
-        pltpu.VMEM((1, count, 3, height, HALF), f32),
+        pltpu.VMEM((count, height, GROUP), f32),
+        pltpu.VMEM((count, 15, height, GROUP), f32),
+        pltpu.VMEM((count, height, GROUP), f32),
+        pltpu.VMEM((count, 3, height, GROUP), f32),
     ]
 
 
@@ -335,20 +385,22 @@
             pltpu.VMEM((2, vocab, HALF), f32),
             pltpu.VMEM((2, vocab, HALF), f32),
             pltpu.VMEM((8, 2, ROWS), f32),
-            pltpu.VMEM((2, 4, HALF), f32),
-            *slots(1, 2),
-            *slots(BISECT_PASSES, 4),
-            *slots(1, 1),
+            pltpu.VMEM((2, 2, HALF), f32),
+            pltpu.VMEM((2, 1, HALF), f32),
+            slots(GROUPS, 2),
+            slots(GROUPS * BISECT_PASSES, 4),
+            slots(GROUPS, 1),
             dma((CHUNKS + 1,)),
             dma((2,)),
             dma((2, UNITS)),
             dma((2, UNITS)),
             dma((2, UNITS)),
+            dma((2, UNITS)),
             dma((2, 4)),
-            dma((2,)),
-            [dma((1, 1))] * 4,
-            [dma((1, BISECT_PASSES))] * 4,
-            [dma((1, 1))] * 4,
+            dma((2, GROUPS + 1)),
+            dma((4, GROUPS)),
+            dma((4, GROUPS * BISECT_PASSES)),
+            dma((4, GROUPS)),
         ],
         compiler_params=pltpu.CompilerParams(
             collective_id=0, has_side_effects=True, vmem_limit_bytes=58 * 1024 * 1024

time: 123 us -> 117 us (0.951)
  Pallas kernels: 118 us -> 112 us
    pallas_call x1, Pallas kernels: 118 us -> 112 us  [on_device(): pl.pallas_call(kernel, out_shape=[jax.ShapeDtypeStruct((vocab, batch), f3...]
where the time goes in v3:
time: 117 us
  Pallas kernels  112 us (96%)
  other arithmetic  4.76 us (4%)
    pallas_call x1, Pallas kernels, on_device(): pl.pallas_call(kernel, out_shape=[jax.ShapeDtypeStruct((vocab, batch), f3...  112 us
    transpose x1, other arithmetic, on_device(): return (out * scale).T  4.76 us

profile of v3, /device:TPU:1, one launch (start us, length us, event | category | flops | bytes accessed | tf_op | source)
XLA Modules:
  0.0 117.0 jit_solution(13830323400272798257)
XLA Ops:
  0.0 112.3 %shard_map.46 = (f32[1010,1024]{1,0:T(8,128)}, f32[1,1024]{1,0:T(1,128)}) custom-call(bf16[128,7168]{1,0:T(8,128)(2,1)} %x_ref.1, bf16[1010,7168]{1,0:T(8,128)(2,1)} %bitcast.7, f32[1,128]{1,0:T(1,128)} %bitcast.8, s32[1,128]{1,0:T(1,128)} %bitcast.9), custom_call_target="tpu_custom_call" | custom-call | flops 14826864640 | bytes 29159424 | tf_op jit(solution)/shard_map/pallas_call | solution.py:376
  112.3 4.8 %multiply_bitcast_fusion = f32[1024,1010]{0,1:T(8,128)} fusion(f32[1010,1024]{1,0:T(8,128)} %get-tuple-element.7, f32[1024]{0:T(1024)} %bitcast.6), kind=kLoop, calls=%fused_computation | loop fusion | flops 1034240 | bytes 8278016 | tf_op jit(solution)/shard_map/transpose | solution.py:412

commit v4 on v3

--- a/solution.py
+++ b/solution.py
@@ -17,15 +17,15 @@
 
 ROWS = 128
 HALF = 512
-GROUP = 256
-GROUPS = 2
+GROUP = 128
+GROUPS = 4
 STRIP = 336
-CHUNKS = 7
+CHUNKS = 4
 UNITS = 4 * CHUNKS
-LAG_FORWARD = 3
-LAG_SHARE = 6
-LAG_MULTIPLY = 8
-EARLY = 4
+LAG_FORWARD = 2
+LAG_SHARE = 4
+LAG_MULTIPLY = 5
+EARLY = 1
 NT = (((1,), (1,)), ((), ()))
 
 
@@ -38,8 +38,10 @@
     plane = [(dp, lax.rem(vo + d, 16)) for d in range(1, 16)]
     column = [(lax.rem(dp + 2 * d, 8), vo) for d in range(1, 4)]
     sibling = (dp + 1 - 2 * lax.rem(dp, 2), vo)
-    others = [(lax.rem(sibling[0] + 2 * d, 8), vo) for d in range(1, 4)]
-    return dp, vo, plane, column, sibling, others
+    x_at, z_at = lax.div(vo, 4), lax.rem(vo, 4)
+    line_z = [(dp, x_at * 4 + lax.rem(z_at + e, 4)) for e in range(1, 4)]
+    line_x = [(dp, lax.rem(x_at + e, 4) * 4 + z_at) for e in range(1, 4)]
+    return dp, x_at, z_at, plane, column, sibling, line_z, line_x
 
 
 def send(src, dst, send_sem, recv_sem, device):
@@ -92,9 +94,10 @@
     x_ref, w_ref, div_ref, quota_ref, out_ref, scale_ref,
     xv, wv, logit, half, expo, rowinfo, final, scale,
     stat_bufs, mass_bufs, kept_bufs,
-    load_sem, row_sem, y_sem, p_sem, f_sem, c_sem, half_sem, final_sem, stat_sem, mass_sem, kept_sem,
+    plane_sem, load_sem, row_sem, y_sem, p_sem, f_sem, c_sem, half_sem, final_sem, stat_sem, mass_sem, kept_sem,
 ):
-    dp, vo, plane, column, sibling, others = places()
+    dp, x_at, z_at, plane, column, sibling, line_z, line_x = places()
+    y_at = lax.div(dp, 2)
     core = lax.rem(dp, 2)
     vocab = w_ref.shape[0]
     depth = w_ref.shape[1]
@@ -108,19 +111,17 @@
         load_w[k].start()
 
     barrier = pltpu.get_barrier_semaphore()
-    greeted = plane + column + [sibling] + others
+    greeted = line_z + line_x + column + [sibling]
     for device in greeted:
         pl.semaphore_signal(barrier, inc=1, device_id=device, device_id_type=MESH)
-    rowinfo[dp] = jnp.concatenate([2.0 / div_ref[...], quota_ref[...].astype(jnp.float32) / 100.0], axis=0)
+    rowinfo[core, y_at] = jnp.concatenate([2.0 / div_ref[...], quota_ref[...].astype(jnp.float32) / 100.0], axis=0)
     pl.semaphore_wait(barrier, len(greeted))
 
-    for device in column + [sibling] + others:
-        send(rowinfo.at[dp], rowinfo.at[dp], row_sem.at[0], row_sem.at[1], device)
-
-    x_at, z_at = lax.div(vo, 4), lax.rem(vo, 4)
-    y_at = lax.div(dp, 2)
-    line_z = [(dp, x_at * 4 + lax.rem(z_at + e, 4)) for e in range(1, 4)]
-    line_x = [(dp, lax.rem(x_at + e, 4) * 4 + z_at) for e in range(1, 4)]
+    for device in line_x:
+        pl.semaphore_signal(plane_sem, inc=1, device_id=device, device_id_type=MESH)
+    for device in column:
+        send(rowinfo.at[core, y_at], rowinfo.at[core, y_at], row_sem.at[0], row_sem.at[1], device)
+
     first_row = pl.multiple_of(dp * ROWS, ROWS)
 
     def unit(m):
@@ -139,7 +140,7 @@
 
     def spread(m, _):
         offset, cols, _ = unit(m)
-        target = (lax.rem(2 * (y_at + 4 - offset) + core, 8), vo)
+        target = (lax.rem(2 * (y_at + 4 - offset) + core, 8), column[0][1])
         for local, there in zip(pieces(0), pieces(dp)):
             send(x_ref.at[local, cols], xv.at[there, cols], y_sem.at[0, m], y_sem.at[1, m], target)
         return 0
@@ -187,11 +188,11 @@
             block = 2 * plane_at + 1 - core
             cols = pl.ds(pl.multiple_of(block * ROWS, ROWS), ROWS)
             there = pl.ds(pl.multiple_of(plane_at * ROWS, ROWS), ROWS)
-            logit[:, cols] = logit[:, cols] * rowinfo[block, 0:1]
+            logit[:, cols] = logit[:, cols] * rowinfo[1 - core, plane_at, 0:1]
             send(logit.at[:, cols], half.at[1, :, there], half_sem.at[0, plane_at], half_sem.at[1, plane_at], sibling)
             block = 2 * plane_at + core
             cols = pl.ds(pl.multiple_of(block * ROWS, ROWS), ROWS)
-            value = logit[:, cols] * rowinfo[block, 0:1]
+            value = logit[:, cols] * rowinfo[core, plane_at, 0:1]
             logit[:, cols] = value
             half[0, :, there] = value
 
@@ -202,8 +203,9 @@
     for m in range(EARLY):
         load_w[m].wait()
         multiply(m)
-    wait_bytes(rowinfo.at[pl.ds(0, 7)], row_sem.at[1])
-    wait_bytes(rowinfo.at[pl.ds(0, 7)], row_sem.at[0])
+    wait_bytes(rowinfo.at[0, pl.ds(0, 3)], row_sem.at[1])
+    wait_bytes(rowinfo.at[0, pl.ds(0, 3)], row_sem.at[0])
+    send(rowinfo.at[core], rowinfo.at[core], row_sem.at[2], row_sem.at[3], sibling)
 
     def step(t, _):
         @pl.when(t < UNITS)
@@ -220,6 +222,10 @@
 
         m = t - LAG_MULTIPLY
 
+        @pl.when(m == EARLY)
+        def _():
+            wait_bytes(rowinfo.at[0], row_sem.at[3])
+
         @pl.when((m >= EARLY) & (m < CHUNKS))
         def _():
             wait_bytes(wv.at[:, pl.ds(0, chunk)], load_sem.at[m])
@@ -231,7 +237,8 @@
         return 0
 
     lax.fori_loop(CHUNKS, UNITS + LAG_MULTIPLY, step, 0)
-    level = jnp.concatenate([rowinfo[2 * j + core, 1:2] for j in range(4)], axis=1)
+    pl.semaphore_wait(plane_sem, 3)
+    level = jnp.concatenate([rowinfo[core, j, 1:2] for j in range(4)], axis=1)
     for j in range(4):
         wait_bytes(half.at[1, :, pl.ds(0, ROWS)], half_sem.at[1, j])
 
@@ -303,7 +310,7 @@
         scale[core, 0:1, lanes] = 1.0 / (total * kept)
 
     def weigh(h, g):
-        for j in (2 * g, 2 * g + 1):
+        for j in range(g * GROUP // ROWS, (g + 1) * GROUP // ROWS):
             lanes = slice(j * ROWS, (j + 1) * ROWS)
             cols = pl.ds(pl.multiple_of((2 * j + h) * ROWS, ROWS), ROWS)
             top, cut = final[h, 0:1, lanes], final[h, 1:2, lanes]
@@ -345,6 +352,7 @@
         return 0
 
     lax.fori_loop(0, UNITS, left, 0)
+    wait_bytes(rowinfo.at[0], row_sem.at[2])
     for j in range(4):
         wait_bytes(half.at[1, :, pl.ds(0, ROWS)], half_sem.at[0, j])
     for g in range(GROUPS):
@@ -384,14 +392,15 @@
             pltpu.VMEM((vocab, batch), f32),
             pltpu.VMEM((2, vocab, HALF), f32),
             pltpu.VMEM((2, vocab, HALF), f32),
-            pltpu.VMEM((8, 2, ROWS), f32),
+            pltpu.VMEM((2, 4, 2, ROWS), f32),
             pltpu.VMEM((2, 2, HALF), f32),
             pltpu.VMEM((2, 1, HALF), f32),
             slots(GROUPS, 2),
             slots(GROUPS * BISECT_PASSES, 4),
             slots(GROUPS, 1),
+            pltpu.SemaphoreType.REGULAR,
             dma((CHUNKS + 1,)),
-            dma((2,)),
+            dma((4,)),
             dma((2, UNITS)),
             dma((2, UNITS)),
             dma((2, UNITS)),

time: 117 us -> 112 us (0.957)
  Pallas kernels: 112 us -> 107 us
    pallas_call x1, Pallas kernels: 112 us -> 107 us  [on_device(): pl.pallas_call(kernel, out_shape=[jax.ShapeDtypeStruct((vocab, batch), f3...]
where the time goes in v4:
time: 112 us
  Pallas kernels  107 us (96%)
  other arithmetic  4.76 us (4%)
    pallas_call x1, Pallas kernels, on_device(): pl.pallas_call(kernel, out_shape=[jax.ShapeDtypeStruct((vocab, batch), f3...  107 us
    transpose x1, other arithmetic, on_device(): return (out * scale).T  4.76 us

profile of v4, /device:TPU:1, one launch (start us, length us, event | category | flops | bytes accessed | tf_op | source)
XLA Modules:
  0.0 112.1 jit_solution(11606013503730790167)
XLA Ops:
  0.0 107.3 %shard_map.46 = (f32[1010,1024]{1,0:T(8,128)}, f32[1,1024]{1,0:T(1,128)}) custom-call(bf16[128,7168]{1,0:T(8,128)(2,1)} %x_ref.1, bf16[1010,7168]{1,0:T(8,128)(2,1)} %bitcast.7, f32[1,128]{1,0:T(1,128)} %bitcast.8, s32[1,128]{1,0:T(1,128)} %bitcast.9), custom_call_target="tpu_custom_call" | custom-call | flops 14826864640 | bytes 29159424 | tf_op jit(solution)/shard_map/pallas_call | solution.py:384
  107.3 4.8 %multiply_bitcast_fusion = f32[1024,1010]{0,1:T(8,128)} fusion(f32[1010,1024]{1,0:T(8,128)} %get-tuple-element.7, f32[1024]{0:T(1024)} %bitcast.6), kind=kLoop, calls=%fused_computation | loop fusion | flops 1034240 | bytes 8278016 | tf_op jit(solution)/shard_map/transpose | solution.py:421

commit v5 on v4

--- a/solution.py
+++ b/solution.py
@@ -19,6 +19,7 @@
 HALF = 512
 GROUP = 128
 GROUPS = 4
+OUT_ROWS = 512
 STRIP = 336
 CHUNKS = 4
 UNITS = 4 * CHUNKS
@@ -92,9 +93,9 @@
 
 def kernel(
     x_ref, w_ref, div_ref, quota_ref, out_ref, scale_ref,
-    xv, wv, logit, half, expo, rowinfo, final, scale,
+    xv, wv, logit, weighed, half, expo, rowinfo, final, scale,
     stat_bufs, mass_bufs, kept_bufs,
-    plane_sem, load_sem, row_sem, y_sem, p_sem, f_sem, c_sem, half_sem, final_sem, stat_sem, mass_sem, kept_sem,
+    plane_sem, load_sem, row_sem, y_sem, p_sem, f_sem, c_sem, half_sem, final_sem, out_sem, stat_sem, mass_sem, kept_sem,
 ):
     dp, x_at, z_at, plane, column, sibling, line_z, line_x = places()
     y_at = lax.div(dp, 2)
@@ -315,7 +316,8 @@
             cols = pl.ds(pl.multiple_of((2 * j + h) * ROWS, ROWS), ROWS)
             top, cut = final[h, 0:1, lanes], final[h, 1:2, lanes]
             value = logit[:, cols]
-            out_ref[:, cols] = jnp.exp(0.5 * (value - top)) * (0.5 + 0.5 * jnp.tanh(value - cut))
+            weighed[:, cols] = jnp.exp(0.5 * (value - top)) * (0.5 + 0.5 * jnp.tanh(value - cut))
+            pltpu.make_async_copy(weighed.at[:, cols], out_ref.at[:, cols], out_sem.at[h, j]).start()
 
     rows_of = [follow(g) for g in range(GROUPS)]
     for _ in range(BISECT_PASSES + 1):
@@ -339,6 +341,11 @@
         lanes = slice(block // 2 * ROWS, (block // 2 + 1) * ROWS)
         scale_ref[:, block * ROWS : (block + 1) * ROWS] = scale[block % 2, :, lanes]
 
+    for h in range(2):
+        for j in range(4):
+            cols = pl.ds((2 * j + h) * ROWS, ROWS)
+            pltpu.make_async_copy(weighed.at[:, cols], out_ref.at[:, cols], out_sem.at[h, j]).wait()
+
     def left(m, _):
         cols = pl.ds(0, chunk)
         wait_bytes(xv.at[pl.ds(0, ROWS), cols], c_sem.at[0, m])
@@ -361,6 +368,10 @@
         for trip in range(in1.shape[0]):
             wait_bytes(in1.at[trip], sems.at[0, trip])
             wait_bytes(in2.at[trip], sems.at[2, trip])
+
+
+def rescale(weight_ref, scale_ref, out_ref):
+    out_ref[...] = weight_ref[...] * scale_ref[...]
 
 
 def slots(count, height):
@@ -385,10 +396,11 @@
         kernel,
         out_shape=[jax.ShapeDtypeStruct((vocab, batch), f32), jax.ShapeDtypeStruct((1, batch), f32)],
         in_specs=[hbm, hbm, vmem, vmem],
-        out_specs=[vmem, vmem],
+        out_specs=[hbm, vmem],
         scratch_shapes=[
             pltpu.VMEM((batch, depth), jnp.bfloat16),
             pltpu.VMEM((vocab, depth), jnp.bfloat16),
+            pltpu.VMEM((vocab, batch), f32),
             pltpu.VMEM((vocab, batch), f32),
             pltpu.VMEM((2, vocab, HALF), f32),
             pltpu.VMEM((2, vocab, HALF), f32),
@@ -407,6 +419,7 @@
             dma((2, UNITS)),
             dma((2, 4)),
             dma((2, GROUPS + 1)),
+            dma((2, 4)),
             dma((4, GROUPS)),
             dma((4, GROUPS * BISECT_PASSES)),
             dma((4, GROUPS)),
@@ -418,7 +431,14 @@
             flops=2 * vocab * depth * batch, bytes_accessed=2 * depth * (vocab + batch), transcendentals=20 * vocab * batch
         ),
     )(latent_vectors, weights, softmax_divisor[None, :], top_probability_quota[None, :])
-    return (out * scale).T
+    block = pl.BlockSpec((OUT_ROWS, batch), lambda i: (i, 0))
+    return pl.pallas_call(
+        rescale,
+        grid=(pl.cdiv(vocab, OUT_ROWS),),
+        out_shape=jax.ShapeDtypeStruct((vocab, batch), f32),
+        in_specs=[block, pl.BlockSpec((1, batch), lambda i: (0, 0))],
+        out_specs=block,
+    )(out, scale).T
 
 
 def solution(mesh):

time: 112 us -> 110 us (0.982)
  other arithmetic: 4.76 us -> 0 us
  Pallas kernels: 107 us -> 110 us
    transpose x1 -> x0, other arithmetic: 4.76 us -> none  [on_device(): return (out * scale).T]
    pallas_call x0 -> x1, Pallas kernels: none -> 3.75 us  [on_device(): pl.pallas_call(rescale, grid=(pl.cdiv(vocab, OUT_ROWS),), out_shape=jax.S...]
    pallas_call x1, Pallas kernels: 107 us -> 106 us  [on_device(): pl.pallas_call(kernel, out_shape=[jax.ShapeDtypeStruct((vocab, batch), f3...]
where the time goes in v5:
time: 110 us
  Pallas kernels  110 us (100%)
    pallas_call x1, Pallas kernels, on_device(): pl.pallas_call(kernel, out_shape=[jax.ShapeDtypeStruct((vocab, batch), f3...  106 us
    pallas_call x1, Pallas kernels, on_device(): pl.pallas_call(rescale, grid=(pl.cdiv(vocab, OUT_ROWS),), out_shape=jax.S...  3.75 us

profile of v5, /device:TPU:1, one launch (start us, length us, event | category | flops | bytes accessed | tf_op | source)
XLA Modules:
  0.0 109.9 jit_solution(10332290951999048046)
XLA Ops:
  0.0 106.1 %shard_map.46 = (f32[1010,1024]{1,0:T(8,128)}, f32[1,1024]{1,0:T(1,128)}) custom-call(bf16[128,7168]{1,0:T(8,128)(2,1)} %x_ref.1, bf16[1010,7168]{1,0:T(8,128)(2,1)} %bitcast.4, f32[1,128]{1,0:T(1,128)} %bitcast.5, s32[1,128]{1,0:T(1,128)} %bitcast.6), custom_call_target="tpu_custom_call" | custom-call | flops 14826864640 | bytes 29159424 | tf_op jit(solution)/shard_map/pallas_call | solution.py:395
  106.1 3.7 %shard_map.47 = f32[1010,1024]{1,0:T(8,128)} custom-call(f32[1010,1024]{1,0:T(8,128)} %get-tuple-element.7.weight_ref, f32[1,1024]{1,0:T(1,128)} %get-tuple-element.8.scale_ref), custom_call_target="tpu_custom_call" | custom-call | tf_op jit(solution)/shard_map/pallas_call | solution.py:435

commit v6 on v5

--- a/solution.py
+++ b/solution.py
@@ -36,10 +36,11 @@
 
 def places():
     dp, vo = lax.axis_index("dp"), lax.axis_index("vocab")
-    plane = [(dp, lax.rem(vo + d, 16)) for d in range(1, 16)]
-    column = [(lax.rem(dp + 2 * d, 8), vo) for d in range(1, 4)]
+    column = [(lax.rem(dp + 2 * d, 8), vo) for d in (2, 1, 3)]
     sibling = (dp + 1 - 2 * lax.rem(dp, 2), vo)
     x_at, z_at = lax.div(vo, 4), lax.rem(vo, 4)
+    steps = sorted(((a, e) for a in range(4) for e in range(4) if a or e), key=lambda s: abs(s[0] - 2) + abs(s[1] - 2))
+    plane = [(dp, lax.rem(x_at + a, 4) * 4 + lax.rem(z_at + e, 4)) for a, e in steps]
     line_z = [(dp, x_at * 4 + lax.rem(z_at + e, 4)) for e in range(1, 4)]
     line_x = [(dp, lax.rem(x_at + e, 4) * 4 + z_at) for e in range(1, 4)]
     return dp, x_at, z_at, plane, column, sibling, line_z, line_x

time: 110 us -> 109 us (level)
  no operation moved by 1% of the time
where the time goes in v6:
time: 109 us
  Pallas kernels  109 us (100%)
    pallas_call x1, Pallas kernels, on_device(): pl.pallas_call(kernel, out_shape=[jax.ShapeDtypeStruct((vocab, batch), f3...  105 us
    pallas_call x1, Pallas kernels, on_device(): pl.pallas_call(rescale, grid=(pl.cdiv(vocab, OUT_ROWS),), out_shape=jax.S...  3.75 us

profile of v6, /device:TPU:1, one launch (start us, length us, event | category | flops | bytes accessed | tf_op | source)
XLA Modules:
  0.0 109.1 jit_solution(11299128959102901306)
XLA Ops:
  0.0 105.3 %shard_map.46 = (f32[1010,1024]{1,0:T(8,128)}, f32[1,1024]{1,0:T(1,128)}) custom-call(bf16[128,7168]{1,0:T(8,128)(2,1)} %x_ref.1, bf16[1010,7168]{1,0:T(8,128)(2,1)} %bitcast.4, f32[1,128]{1,0:T(1,128)} %bitcast.5, s32[1,128]{1,0:T(1,128)} %bitcast.6), custom_call_target="tpu_custom_call" | custom-call | flops 14826864640 | bytes 29159424 | tf_op jit(solution)/shard_map/pallas_call | solution.py:396
  105.3 3.7 %shard_map.47 = f32[1010,1024]{1,0:T(8,128)} custom-call(f32[1010,1024]{1,0:T(8,128)} %get-tuple-element.7.weight_ref, f32[1,1024]{1,0:T(1,128)} %get-tuple-element.8.scale_ref), custom_call_target="tpu_custom_call" | custom-call | tf_op jit(solution)/shard_map/pallas_call | solution.py:436
